TPU v7x, 32 devices: a whole 2x2x4 slice. The times are simulated.
32 devices in a mesh: slab: 8 (over z, y), leaf: 4 (over x, core).
Axes of the slice: x: 2, y: 2, z: 4, core: 2. Of those that a mesh axis runs over, the one named last changes fastest.
Arguments:
- probes: bfloat16 [16384, 128], P(('slab', 'leaf')), may hold values from -6 to 6
- near_blocks: bfloat16 [32, 3, 512, 512], P(('slab', 'leaf')), may hold values from -0.15625 to 0.15625
- near_offsets: int32 [32, 3], P(('slab', 'leaf')), may hold values from -1 to 1
- far_basis: bfloat16 [5, 16384, 128], P(None, ('slab', 'leaf')), may hold values from -0.25 to 0.25
Outputs:
- product: float32 [16384, 128], P(('slab', 'leaf'))
Inputs may be any that keep to these rules, and one draw needn't show every extreme that they name: `near_offsets`: offsets that point outside the leaves meet zero probes.
All inputs are finite; a program needn't handle non-finite values.
Results may differ from a plain program's by a relative error of at most 0.0025.
Values may be sent and summed in bfloat16 or wider, within the bound.
A program may use at most 64 MiB of HBM per device.

v0:
```python
import jax
import jax.numpy as jnp
from jax import lax
from jax.sharding import PartitionSpec as P


def extended(block, sides, width):
    for axis, dim in sides:
        count = lax.axis_size(axis)
        forward = [(i, i + 1) for i in range(count - 1)]
        backward = [(target, source) for source, target in forward]
        low = lax.ppermute(
            lax.slice_in_dim(block, block.shape[dim] - width, None, axis=dim), axis, forward
        )
        high = lax.ppermute(lax.slice_in_dim(block, 0, width, axis=dim), axis, backward)
        block = jnp.concatenate([low, block, high], axis=dim)
    return block


def swapped(value, axis, bit):
    mask = 2**bit
    pairs = [(source, source ^ mask) for source in range(lax.axis_size(axis))]
    return lax.ppermute(value, axis, pairs)


def body(probes, near_blocks, near_offsets, far_basis):
    leaf_rows = probes.shape[0]
    levels = far_basis.shape[0]
    padded = extended(probes, ((("slab", "leaf"), 0),), leaf_rows)
    near_sum = jnp.zeros(probes.shape, jnp.float32)
    for member in range(near_blocks.shape[1]):
        window_start = (near_offsets[0, member] + 1) * leaf_rows
        window = lax.dynamic_slice_in_dim(padded, window_start, leaf_rows, 0)
        near_sum = near_sum + jnp.dot(
            near_blocks[0, member], window, preferred_element_type=jnp.float32
        )
    projected = jnp.einsum("lpr,pq->lrq", far_basis, probes, preferred_element_type=jnp.float32)
    leaf_bits = lax.axis_size("leaf").bit_length() - 1
    sibling = [None] * levels
    partial_sums = [projected[level] for level in range(levels)]
    for tree_bit in range(leaf_bits):
        incoming = swapped(jnp.stack(partial_sums[tree_bit:]), "leaf", tree_bit)
        sibling[tree_bit] = incoming[0]
        for level in range(tree_bit + 1, levels):
            partial_sums[level] = partial_sums[level] + incoming[level - tree_bit]
    for tree_bit in range(levels - leaf_bits):
        level_now = leaf_bits + tree_bit
        incoming = swapped(jnp.stack(partial_sums[level_now:]), "slab", tree_bit)
        sibling[level_now] = incoming[0]
        for level in range(level_now + 1, levels):
            partial_sums[level] = partial_sums[level] + incoming[level - level_now]
    output = near_sum
    for level in range(levels):
        coupling = (sibling[level] * 2.0 ** (-0.5 * level)).astype(jnp.bfloat16)
        output = output + jnp.dot(far_basis[level], coupling, preferred_element_type=jnp.float32)
    return output


def solution(mesh):
    return jax.shard_map(
        body,
        mesh=mesh,
        in_specs=(
            P(("slab", "leaf"), None),
            P(("slab", "leaf"), None, None, None),
            P(("slab", "leaf"), None),
            P(None, ("slab", "leaf"), None),
        ),
        out_specs=P(("slab", "leaf"), None),
        check_vma=False,
    )
```

profile of v0, /device:TPU:0, one launch (start us, length us, event | category | flops | bytes accessed | tf_op | source)
XLA Modules:
  0.0 41.6 jit_solution(12149150913017901956)
XLA Ops:
  0.0 0.0 copy-start.1
  0.0 2.5 %collective-permute-start = (bf16[512,128]{1,0:T(8,128)(2,1)}, bf16[512,128]{1,0:T(8,128)(2,1)S(1)}, u32[]{:S(2)}, u32[]{:S(2)}) collective-permute-start(bf16[512,128]{1,0:T(8,128)(2,1)} %param.4), channel_id=1, source_target_pairs={{0,1},{1,2},{2,3},{3,4},{4,5},{5,6},{6,7},{7,8},{8,9},{9,10},{10,1... | collective-permute-start | bytes 393224 | tf_op jit(solution)/shard_map/ppermute | solution.py:12
  2.5 1.3 %collective-permute-start.1 = (bf16[512,128]{1,0:T(8,128)(2,1)}, bf16[512,128]{1,0:T(8,128)(2,1)S(1)}, u32[]{:S(2)}, u32[]{:S(2)}) collective-permute-start(bf16[512,128]{1,0:T(8,128)(2,1)} %param.4), channel_id=1, source_target_pairs={{1,0},{2,1},{3,2},{4,3},{5,4},{6,5},{7,6},{8,7},{9,8},{10,9},{11,1... | collective-permute-start | bytes 393224 | tf_op jit(solution)/shard_map/ppermute | solution.py:15
  3.8 1.5 %fusion.19 = f32[5,128,128]{2,1,0:T(8,128)S(1)} fusion(bf16[5,512,128]{2,1,0:T(8,128)(2,1)} %param.7, bf16[512,128]{1,0:T(8,128)(2,1)} %param.4), kind=kOutput, calls=%fused_computation.26 | convolution fusion | flops 83886080 | bytes 1114112 | tf_op jit(solution)/shard_map/lpr,pq->lrq/dot_general | solution.py:37
  5.3 3.3 %collective-permute-start.2 = (f32[5,128,128]{2,1,0:T(8,128)S(1)}, f32[5,128,128]{2,1,0:T(8,128)S(1)}, u32[]{:S(2)}, u32[]{:S(2)}) collective-permute-start(f32[5,128,128]{2,1,0:T(8,128)S(1)} %fusion.19), channel_id=1, source_target_pairs={{0,1},{1,0},{2,3},{3,2},{4,5},{5,4},{6,7},{7,6},{8,9},{9,8},{10,11... | collective-permute-start | bytes 983048 | tf_op jit(solution)/shard_map/ppermute | solution.py:23
  8.6 1.4 %fusion.53 = (s32[1,1]{1,0:T(1,128)}, s32[1,1]{1,0:T(1,128)}, s32[1,1]{1,0:T(1,128)}) fusion(s32[1,3]{1,0:T(1,128)} %param.6), kind=kLoop, calls=%fused_computation.73 | loop fusion | bytes 24 | tf_op jit(solution)/shard_map/slice | solution.py:32
  11.8 0.0 collective-permute-done
  11.8 0.9 %constant_dynamic-update-slice_fusion.1 = bf16[1536,128]{1,0:T(8,128)(2,1)S(1)} fusion(bf16[1536,128]{1,0:T(8,128)(2,1)S(1)} %constant_dynamic-update-slice_fusion.2, bf16[512,128]{1,0:T(8,128)(2,1)} %param.4), kind=kLoop, calls=%fused_computation.64 | loop fusion | bytes 262144
  12.8 0.0 collective-permute-done.1
  12.8 0.0 copy-done.1
  12.8 0.0 copy-start
  12.8 0.3 fusion.4
  13.1 0.0 collective-permute-done.2
  13.2 1.7 %collective-permute-start.3 = (f32[4,128,128]{2,1,0:T(8,128)S(1)}, f32[4,128,128]{2,1,0:T(8,128)S(1)}, u32[]{:S(2)}, u32[]{:S(2)}) collective-permute-start(f32[4,128,128]{2,1,0:T(8,128)S(1)} %pad_maximum_fusion), channel_id=1, source_target_pairs={{0,2},{1,3},{2,0},{3,1},{4,6},{5,7},{6,4},{7,5},{8,10},{9,11},{10,... | collective-permute-start | bytes 786440 | tf_op jit(solution)/shard_map/ppermute | solution.py:23
  14.9 0.3 fusion.6
  15.2 0.0 copy-done
  15.2 0.2 fusion.17
  15.5 6.4 %collective-permute-done.3 = f32[4,128,128]{2,1,0:T(8,128)S(1)} collective-permute-done((f32[4,128,128]{2,1,0:T(8,128)S(1)}, f32[4,128,128]{2,1,0:T(8,128)S(1)}, u32[]{:S(2)}, u32[]{:S(2)}) %collective-permute-start.3) | collective-permute-done | bytes 262176 | tf_op jit(solution)/shard_map/ppermute | solution.py:23
  21.9 2.7 %collective-permute-start.4 = (f32[3,128,128]{2,1,0:T(8,128)S(1)}, f32[3,128,128]{2,1,0:T(8,128)S(1)}, u32[]{:S(2)}, u32[]{:S(2)}) collective-permute-start(f32[3,128,128]{2,1,0:T(8,128)S(1)} %pad_maximum_fusion.1), channel_id=1, source_target_pairs={{0,4},{4,0},{8,12},{12,8},{16,20},{20,16},{24,28},{28,24},{1,5},{5... | collective-permute-start | bytes 589832 | tf_op jit(solution)/shard_map/ppermute | solution.py:23
  24.7 0.2 fusion.15
  24.9 0.3 fusion.3
  25.2 4.2 %collective-permute-done.4 = f32[3,128,128]{2,1,0:T(8,128)S(1)} collective-permute-done((f32[3,128,128]{2,1,0:T(8,128)S(1)}, f32[3,128,128]{2,1,0:T(8,128)S(1)}, u32[]{:S(2)}, u32[]{:S(2)}) %collective-permute-start.4) | collective-permute-done | bytes 196640 | tf_op jit(solution)/shard_map/ppermute | solution.py:23
  29.5 2.8 %collective-permute-start.5 = (f32[2,128,128]{2,1,0:T(8,128)S(1)}, f32[2,128,128]{2,1,0:T(8,128)S(1)}, u32[]{:S(2)}, u32[]{:S(2)}) collective-permute-start(f32[2,128,128]{2,1,0:T(8,128)S(1)} %pad_maximum_fusion.2), channel_id=1, source_target_pairs={{0,8},{4,12},{8,0},{12,4},{16,24},{20,28},{24,16},{28,20},{1,9},{5... | collective-permute-start | bytes 393224 | tf_op jit(solution)/shard_map/ppermute | solution.py:23
  32.2 0.2 convolution_add_fusion.2
  32.5 2.7 %collective-permute-done.5 = f32[2,128,128]{2,1,0:T(8,128)S(1)} collective-permute-done((f32[2,128,128]{2,1,0:T(8,128)S(1)}, f32[2,128,128]{2,1,0:T(8,128)S(1)}, u32[]{:S(2)}, u32[]{:S(2)}) %collective-permute-start.5) | collective-permute-done | bytes 131104 | tf_op jit(solution)/shard_map/ppermute | solution.py:23
  35.2 3.1 %collective-permute-start.6 = (f32[1,128,128]{2,1,0:T(8,128)S(1)}, f32[1,128,128]{2,1,0:T(8,128)S(1)}, u32[]{:S(2)}, u32[]{:S(2)}) collective-permute-start(f32[1,128,128]{2,1,0:T(8,128)S(1)} %slice_add_fusion), channel_id=1, source_target_pairs={{0,16},{4,20},{8,24},{12,28},{16,0},{20,4},{24,8},{28,12},{1,17},{... | collective-permute-start | bytes 196616 | tf_op jit(solution)/shard_map/ppermute | solution.py:23
  38.3 0.2 convolution_add_fusion.1
  38.5 2.0 %collective-permute-done.6 = f32[1,128,128]{2,1,0:T(8,128)S(1)} collective-permute-done((f32[1,128,128]{2,1,0:T(8,128)S(1)}, f32[1,128,128]{2,1,0:T(8,128)S(1)}, u32[]{:S(2)}, u32[]{:S(2)}) %collective-permute-start.6) | collective-permute-done | bytes 65568 | tf_op jit(solution)/shard_map/ppermute | solution.py:23
  40.5 0.2 fusion
  40.8 0.8 %copy.6 = f32[512,128]{1,0:T(8,128)} copy(f32[512,128]{0,1:T(8,128)S(1)} %fusion) | data formatting | bytes 524288 | tf_op jit(solution)/shard_map/add | solution.py:55
  (9 shorter events, 0.2 us)
Async XLA Ops:
  0.0 12.8 %copy-start.1 = (bf16[1,3,512,512]{3,2,1,0:T(8,128)(2,1)S(1)}, bf16[1,3,512,512]{3,2,1,0:T(8,128)(2,1)}, u32[]{:S(2)}) copy-start(bf16[1,3,512,512]{3,2,1,0:T(8,128)(2,1)} %param.5) | copy-start | bytes 4718596
  0.0 11.8 %collective-permute-start = (bf16[512,128]{1,0:T(8,128)(2,1)}, bf16[512,128]{1,0:T(8,128)(2,1)S(1)}, u32[]{:S(2)}, u32[]{:S(2)}) collective-permute-start(bf16[512,128]{1,0:T(8,128)(2,1)} %param.4), channel_id=1, source_target_pairs={{0,1},{1,2},{2,3},{3,4},{4,5},{5,6},{6,7},{7,8},{8,9},{9,10},{10,1... | collective-permute-start | bytes 393224 | tf_op jit(solution)/shard_map/ppermute | solution.py:12
  2.5 10.3 %collective-permute-start.1 = (bf16[512,128]{1,0:T(8,128)(2,1)}, bf16[512,128]{1,0:T(8,128)(2,1)S(1)}, u32[]{:S(2)}, u32[]{:S(2)}) collective-permute-start(bf16[512,128]{1,0:T(8,128)(2,1)} %param.4), channel_id=1, source_target_pairs={{1,0},{2,1},{3,2},{4,3},{5,4},{6,5},{7,6},{8,7},{9,8},{10,9},{11,1... | collective-permute-start | bytes 393224 | tf_op jit(solution)/shard_map/ppermute | solution.py:15
  5.3 7.9 %collective-permute-start.2 = (f32[5,128,128]{2,1,0:T(8,128)S(1)}, f32[5,128,128]{2,1,0:T(8,128)S(1)}, u32[]{:S(2)}, u32[]{:S(2)}) collective-permute-start(f32[5,128,128]{2,1,0:T(8,128)S(1)} %fusion.19), channel_id=1, source_target_pairs={{0,1},{1,0},{2,3},{3,2},{4,5},{5,4},{6,7},{7,6},{8,9},{9,8},{10,11... | collective-permute-start | bytes 983048 | tf_op jit(solution)/shard_map/ppermute | solution.py:23
  12.8 2.4 %copy-start = (bf16[5,512,128]{2,1,0:T(8,128)(2,1)S(1)}, bf16[5,512,128]{2,1,0:T(8,128)(2,1)}, u32[]{:S(2)}) copy-start(bf16[5,512,128]{2,1,0:T(8,128)(2,1)} %param.7) | copy-start | bytes 1966084
  13.2 8.7 %collective-permute-start.3 = (f32[4,128,128]{2,1,0:T(8,128)S(1)}, f32[4,128,128]{2,1,0:T(8,128)S(1)}, u32[]{:S(2)}, u32[]{:S(2)}) collective-permute-start(f32[4,128,128]{2,1,0:T(8,128)S(1)} %pad_maximum_fusion), channel_id=1, source_target_pairs={{0,2},{1,3},{2,0},{3,1},{4,6},{5,7},{6,4},{7,5},{8,10},{9,11},{10,... | collective-permute-start | bytes 786440 | tf_op jit(solution)/shard_map/ppermute | solution.py:23
  21.9 7.5 %collective-permute-start.4 = (f32[3,128,128]{2,1,0:T(8,128)S(1)}, f32[3,128,128]{2,1,0:T(8,128)S(1)}, u32[]{:S(2)}, u32[]{:S(2)}) collective-permute-start(f32[3,128,128]{2,1,0:T(8,128)S(1)} %pad_maximum_fusion.1), channel_id=1, source_target_pairs={{0,4},{4,0},{8,12},{12,8},{16,20},{20,16},{24,28},{28,24},{1,5},{5... | collective-permute-start | bytes 589832 | tf_op jit(solution)/shard_map/ppermute | solution.py:23
  29.5 5.7 %collective-permute-start.5 = (f32[2,128,128]{2,1,0:T(8,128)S(1)}, f32[2,128,128]{2,1,0:T(8,128)S(1)}, u32[]{:S(2)}, u32[]{:S(2)}) collective-permute-start(f32[2,128,128]{2,1,0:T(8,128)S(1)} %pad_maximum_fusion.2), channel_id=1, source_target_pairs={{0,8},{4,12},{8,0},{12,4},{16,24},{20,28},{24,16},{28,20},{1,9},{5... | collective-permute-start | bytes 393224 | tf_op jit(solution)/shard_map/ppermute | solution.py:23
  35.2 5.3 %collective-permute-start.6 = (f32[1,128,128]{2,1,0:T(8,128)S(1)}, f32[1,128,128]{2,1,0:T(8,128)S(1)}, u32[]{:S(2)}, u32[]{:S(2)}) collective-permute-start(f32[1,128,128]{2,1,0:T(8,128)S(1)} %slice_add_fusion), channel_id=1, source_target_pairs={{0,16},{4,20},{8,24},{12,28},{16,0},{20,4},{24,8},{28,12},{1,17},{... | collective-permute-start | bytes 196616 | tf_op jit(solution)/shard_map/ppermute | solution.py:23
where the time goes:
time: 41.9 us; the launch traced here: 41.6 us
  starting transfers between devices  17.4 us (42%)
  waiting for transfers between devices  15.4 us (37%)
  matrix products  3.45 us (8%)
  local copies, waits for them, and re-layouts  3.18 us (8%)
  between operations  2.06 us (5%)
    ppermute x5, waiting for transfers between devices, swapped(): return lax.ppermute(value, axis, pairs)  15.4 us
    ppermute x5, starting transfers between devices, swapped(): return lax.ppermute(value, axis, pairs)  13.6 us
    ppermute x1, starting transfers between devices, extended(): lax.ppermute(lax.slice_in_dim(block, block.shape[dim] - width, None, axis...  2.49 us
    dot_general x1, matrix products, body(): jnp.einsum('lpr,pq->lrq', far_basis, probes, preferred_element_type=jnp.f...  1.47 us
    slice x1, local copies, waits for them, and re-layouts, body(): window_start = (near_offsets[0, member] + 1) * leaf_rows  1.37 us
    ppermute x1, starting transfers between devices, extended(): lax.ppermute(lax.slice_in_dim(block, 0, width, axis=dim), axis, backward)  1.29 us
    dot_general x5, matrix products, body(): jnp.dot(far_basis[level], coupling, preferred_element_type=jnp.float32)  1.03 us
    dot_general x3, matrix products, body(): jnp.dot(near_blocks[0, member], window, preferred_element_type=jnp.float32)  0.95 us
  transfers between devices with their start and end apart: 7, of which 4 were waited for; matrix products, arithmetic and copies ran while one was open for 13% of the time, Pallas kernels for 0%

commit v1 on v0

v1 whole, which is shorter than its diff:
```python
import functools

import jax
import jax.numpy as jnp
from jax import lax
from jax.experimental import pallas as pl
from jax.experimental.pallas import tpu as pltpu
from jax.sharding import PartitionSpec as P

MESH = pl.DeviceIdType.MESH
DIRECT_LEVELS = 5


def flipped(index, mask):
    bit = 1
    result = index
    while bit <= mask:
        if mask & bit:
            result = result + bit * (1 - 2 * ((index // bit) % 2))
        bit *= 2
    return result


def owner_parity(level):
    return None if level < 3 else level % 2


def owner_count(level):
    return 2**level if level < 3 else 2 ** (level - 1)


def kernel(
    levels, slabs, leaves, offsets, probes_hbm, near_hbm, far_hbm, out_hbm,
    window, near, far, partial, arrived, piece, coupling, out,
    load_sem, out_sem, sum_send, sum_recv, piece_send, piece_recv, probe_send, probe_recv,
):
    slab, leaf = lax.axis_index("slab"), lax.axis_index("leaf")
    me = slab * leaves + leaf
    core = leaf % 2
    total = slabs * leaves
    group = 2**levels
    rank = partial.shape[1]
    points = window.shape[1]

    def device(mask):
        return flipped(slab, mask // leaves), flipped(leaf, mask % leaves)

    def along(step):
        other = me + step
        return other // leaves, other % leaves

    load_probes = pltpu.make_async_copy(probes_hbm, window.at[1], load_sem.at[0])
    load_far = pltpu.make_async_copy(far_hbm.at[pl.ds(0, levels)], far, load_sem.at[1])
    load_near = pltpu.make_async_copy(near_hbm.at[0], near, load_sem.at[2])
    load_probes.start()
    load_far.start()
    load_near.start()

    has_low, has_high = me > 0, me < total - 1
    barrier = pltpu.get_barrier_semaphore()
    for mask in range(1, group):
        pl.semaphore_signal(barrier, inc=1, device_id=device(mask), device_id_type=MESH)
    if total > group:
        low_outside = jnp.logical_and(has_low, me % group == 0)
        high_outside = jnp.logical_and(has_high, me % group == group - 1)
        for outside, step in ((low_outside, -1), (high_outside, 1)):
            @pl.when(outside)
            def _():
                pl.semaphore_signal(barrier, inc=1, device_id=along(step), device_id_type=MESH)

    load_probes.wait()
    load_far.wait()
    turned = window[1].T
    for level in reversed(range(levels)):
        partial[level] = jnp.dot(turned, far[level], preferred_element_type=jnp.float32)
    piece[0] = partial[0].astype(jnp.bfloat16)

    pl.semaphore_wait(barrier, group - 1)
    if total > group:
        for outside in (low_outside, high_outside):
            @pl.when(outside)
            def _():
                pl.semaphore_wait(barrier, 1)

    def remote(source, target, send, recv, where):
        return pltpu.make_async_remote_copy(
            src_ref=source, dst_ref=target, send_sem=send, recv_sem=recv,
            device_id=where, device_id_type=MESH,
        )

    def rows_of(level, index):
        count = owner_count(level)
        chunk = index % 2**level
        if owner_parity(level) is not None:
            chunk = chunk // 2
        height = rank // count
        return pl.ds(pl.multiple_of(chunk * height, height), height)

    for level in reversed(range(1, levels)):
        parity = owner_parity(level)
        if parity is None:
            for mask in range(1, 2**level):
                where = device(mask)
                remote(
                    partial.at[level, rows_of(level, flipped(me, mask))],
                    arrived[level - 1].at[mask],
                    sum_send.at[level], sum_recv.at[level], where,
                ).start()
        else:
            differs = (core + parity) % 2
            for pair in reversed(range(2 ** (level - 1))):
                where_slab, where_leaf = device(2 * pair)
                where = where_slab, where_leaf - core + parity
                index = where[0] * leaves + where[1]

                def send():
                    remote(
                        partial.at[level, rows_of(level, index)],
                        arrived[level - 1].at[2 * pair + differs],
                        sum_send.at[level], sum_recv.at[level], where,
                    ).start()

                if pair == 0:
                    pl.when(differs == 1)(send)
                else:
                    send()

    remote(piece.at[0], coupling.at[0], piece_send.at[0], piece_recv.at[0], device(1)).start()

    to_low = remote(window.at[1], window.at[2], probe_send.at[0], probe_recv.at[1], along(-1))
    to_high = remote(window.at[1], window.at[0], probe_send.at[1], probe_recv.at[0], along(1))
    pl.when(has_low)(to_low.start)
    pl.when(has_high)(to_high.start)

    def await_bytes(ref, sem):
        pltpu.make_async_copy(ref, ref, sem).wait()

    def finish(level):
        rows = rows_of(level, me)
        height = rank // owner_count(level)
        members = 2**level
        await_bytes(arrived[level - 1].at[pl.ds(1, members - 1)], sum_recv.at[level])
        value = partial[level, rows]
        for member in range(1, members):
            value = value + arrived[level - 1][member]
        value = (value * 2.0 ** (-0.5 * level)).astype(jnp.bfloat16)
        piece[level, pl.ds(0, height)] = value
        for mask in reversed(range(members, 2 * members)):
            remote(
                piece.at[level, pl.ds(0, height)], coupling.at[level, rows],
                piece_send.at[level], piece_recv.at[level], device(mask),
            ).start()

    for level in reversed(range(1, levels)):
        parity = owner_parity(level)
        if parity is None:
            finish(level)
        else:
            pl.when(core == parity)(functools.partial(finish, level))

    @pl.when(jnp.logical_not(has_low))
    def _():
        window[0] = jnp.zeros_like(window[0])

    @pl.when(jnp.logical_not(has_high))
    def _():
        window[2] = jnp.zeros_like(window[2])

    pl.when(has_high)(lambda: await_bytes(window.at[2], probe_recv.at[1]))
    pl.when(has_low)(lambda: await_bytes(window.at[0], probe_recv.at[0]))
    load_near.wait()
    members = near.shape[0]
    value = jnp.dot(near[0], window[offsets[0, 0] + 1], preferred_element_type=jnp.float32)
    for member in range(1, members):
        value = value + jnp.dot(
            near[member], window[offsets[0, member] + 1], preferred_element_type=jnp.float32
        )
    out[...] = value

    for level in range(levels):
        await_bytes(coupling.at[level], piece_recv.at[level])
    value = out[...]
    for level in range(levels):
        value = value + lax.dot_general(
            far[level], coupling[level], (((1,), (1,)), ((), ())),
            preferred_element_type=jnp.float32,
        )
    out[...] = value
    store = pltpu.make_async_copy(out, out_hbm, out_sem)
    store.start()

    await_bytes(piece.at[0], piece_send.at[0])
    for level in range(1, levels):
        parity = owner_parity(level)
        height = rank // owner_count(level)
        if parity is None:
            await_bytes(partial.at[level, pl.ds(0, rank - height)], sum_send.at[level])
            await_bytes(coupling.at[level], piece_send.at[level])
        else:
            @pl.when(core == parity)
            def _():
                await_bytes(partial.at[level, pl.ds(0, rank - height)], sum_send.at[level])
                await_bytes(coupling.at[pl.ds(0, 2)], piece_send.at[level])

            @pl.when(core != parity)
            def _():
                await_bytes(partial.at[level], sum_send.at[level])

    pl.when(has_low)(to_low.wait_send)
    pl.when(has_high)(to_high.wait_send)
    store.wait()


def direct(probes, near_blocks, near_offsets, far_basis, levels):
    points, columns = probes.shape
    rank = far_basis.shape[2]
    members = near_blocks.shape[1]
    slabs, leaves = lax.axis_size("slab"), lax.axis_size("leaf")
    arrived = [
        pltpu.VMEM((2**level, rank // owner_count(level), columns), jnp.float32)
        for level in range(1, levels)
    ]
    flops = 2 * points * columns * (members * points + 2 * levels * rank)
    return pl.pallas_call(
        functools.partial(kernel, levels, slabs, leaves),
        out_shape=jax.ShapeDtypeStruct((points, columns), jnp.float32),
        in_specs=[pl.BlockSpec(memory_space=pltpu.SMEM)] + [pl.BlockSpec(memory_space=pl.ANY)] * 3,
        out_specs=pl.BlockSpec(memory_space=pl.ANY),
        scratch_shapes=[
            pltpu.VMEM((3, points, columns), jnp.bfloat16),
            pltpu.VMEM((members, points, points), jnp.bfloat16),
            pltpu.VMEM((levels, points, rank), jnp.bfloat16),
            pltpu.VMEM((levels, columns, rank), jnp.float32),
            arrived,
            pltpu.VMEM((levels, columns, rank), jnp.bfloat16),
            pltpu.VMEM((levels, columns, rank), jnp.bfloat16),
            pltpu.VMEM((points, columns), jnp.float32),
            pltpu.SemaphoreType.DMA((3,)),
            pltpu.SemaphoreType.DMA,
            pltpu.SemaphoreType.DMA((levels,)),
            pltpu.SemaphoreType.DMA((levels,)),
            pltpu.SemaphoreType.DMA((levels,)),
            pltpu.SemaphoreType.DMA((levels,)),
            pltpu.SemaphoreType.DMA((2,)),
            pltpu.SemaphoreType.DMA((2,)),
        ],
        compiler_params=pltpu.CompilerParams(
            collective_id=0, has_side_effects=True, vmem_limit_bytes=24 * 2**20
        ),
        cost_estimate=pl.CostEstimate(flops=flops, bytes_accessed=2 * near_blocks.size, transcendentals=0),
    )(near_offsets, probes, near_blocks, far_basis)


def swapped(value, axis, bit):
    mask = 2**bit
    pairs = [(source, source ^ mask) for source in range(lax.axis_size(axis))]
    return lax.ppermute(value, axis, pairs)


def upper(output, probes, far_basis, first):
    levels = far_basis.shape[0]
    partial_sums = {
        level: lax.dot_general(
            far_basis[level], probes, (((0,), (0,)), ((), ())), preferred_element_type=jnp.float32
        )
        for level in range(first, levels)
    }
    leaf_bits = lax.axis_size("leaf").bit_length() - 1
    for bit in range(levels):
        axis, axis_bit = ("leaf", bit) if bit < leaf_bits else ("slab", bit - leaf_bits)
        kept = [level for level in range(first, levels) if level >= bit]
        incoming = swapped(jnp.stack([partial_sums[level] for level in kept]), axis, axis_bit)
        for place, level in enumerate(kept):
            if level == bit:
                coupling = (incoming[place] * 2.0 ** (-0.5 * level)).astype(jnp.bfloat16)
                output = output + jnp.dot(
                    far_basis[level], coupling, preferred_element_type=jnp.float32
                )
            else:
                partial_sums[level] = partial_sums[level] + incoming[place]
    return output


def body(probes, near_blocks, near_offsets, far_basis):
    levels = far_basis.shape[0]
    first = min(levels, DIRECT_LEVELS)
    output = direct(probes, near_blocks, near_offsets, far_basis, first)
    if levels > first:
        output = upper(output, probes, far_basis, first)
    return output


def solution(mesh):
    return jax.shard_map(
        body,
        mesh=mesh,
        in_specs=(
            P(("slab", "leaf"), None),
            P(("slab", "leaf"), None, None, None),
            P(("slab", "leaf"), None),
            P(None, ("slab", "leaf"), None),
        ),
        out_specs=P(("slab", "leaf"), None),
        check_vma=False,
    )
```

time: 41.9 us -> 22.9 us (0.55)
  Pallas kernels: 0 us -> 18 us
  starting transfers between devices: 17.4 us -> 0 us
  waiting for transfers between devices: 15.4 us -> 0 us
  matrix products: 3.45 us -> 0 us
  between operations: 2.06 us -> 0.01 us
  local copies, waits for them, and re-layouts: 3.18 us -> 4.76 us
    pallas_call x0 -> x1, Pallas kernels: none -> 18 us  [direct(): pl.pallas_call(functools.partial(kernel, levels, slabs, leaves), out_shap...]
    ppermute x7 -> x0, starting transfers between devices: 17.4 us -> none  [the longest x5 13.6 us: swapped(): return lax.ppermute(value, axis, pairs)]
    ppermute x7 -> x0, waiting for transfers between devices: 15.4 us -> none  [the longest x5 15.4 us: swapped(): return lax.ppermute(value, axis, pairs)]
    unnamed x6 -> x9, local copies, waits for them, and re-layouts: 0.94 us -> 4.76 us
    dot_general x9 -> x0, matrix products: 3.45 us -> none  [the longest x1 1.47 us: body(): jnp.einsum('lpr,pq->lrq', far_basis, probes, preferred_element_type=jnp.f...]
    slice x1 -> x0, local copies, waits for them, and re-layouts: 1.37 us -> none  [body(): window_start = (near_offsets[0, member] + 1) * leaf_rows]
    add x1 -> x0, local copies, waits for them, and re-layouts: 0.84 us -> none  [body(): output + jnp.dot(far_basis[level], coupling, preferred_element_type=jnp.f...]
  transfers between devices with their start and end apart: 7 -> 0, of which waited for: 4 -> 0; matrix products, arithmetic and copies ran while one was open for 13% -> 0% of each run, Pallas kernels for 0% -> 0%
where the time goes in v1:
time: 22.9 us; the launch traced here: 22.7 us
  Pallas kernels  18 us (79%)
  local copies, waits for them, and re-layouts  4.76 us (21%)
    pallas_call x1, Pallas kernels, direct(): pl.pallas_call(functools.partial(kernel, levels, slabs, leaves), out_shap...  18 us
    unnamed x9, local copies, waits for them, and re-layouts  4.76 us

profile of v1, /device:TPU:0, one launch (start us, length us, event | category | flops | bytes accessed | tf_op | source)
XLA Modules:
  0.0 22.7 jit_solution(3848081589005350631)
XLA Ops:
  0.0 0.0 copy-start
  0.0 1.4 %copy-done = bf16[1,3,512,512]{3,2,1,0:T(8,128)(2,1)S(1)} copy-done((bf16[1,3,512,512]{3,2,1,0:T(8,128)(2,1)S(1)}, bf16[1,3,512,512]{3,2,1,0:T(8,128)(2,1)}, u32[]{:S(2)}) %copy-start) | copy-done | bytes 1572888
  1.4 0.0 copy-start.1
  1.4 1.1 %copy-done.1 = bf16[5,512,128]{2,1,0:T(8,128)(2,1)S(1)} copy-done((bf16[5,512,128]{2,1,0:T(8,128)(2,1)S(1)}, bf16[5,512,128]{2,1,0:T(8,128)(2,1)}, u32[]{:S(2)}) %copy-start.1) | copy-done | bytes 655384
  2.5 0.0 copy-start.2
  2.5 0.9 %copy-done.2 = bf16[512,128]{1,0:T(8,128)(2,1)S(1)} copy-done((bf16[512,128]{1,0:T(8,128)(2,1)S(1)}, bf16[512,128]{1,0:T(8,128)(2,1)}, u32[]{:S(2)}) %copy-start.2) | copy-done | bytes 131096
  3.4 0.0 copy-start.3
  3.4 0.7 %copy-done.3 = s32[1,3]{1,0:T(1,128)S(1)} copy-done((s32[1,3]{1,0:T(1,128)S(1)}, s32[1,3]{1,0:T(1,128)}, u32[]{:S(2)}) %copy-start.3) | copy-done | bytes 36
  4.1 18.0 %shard_map.46 = f32[512,128]{1,0:T(8,128)S(1)} custom-call(s32[1,3]{1,0:T(1,128)S(1)} %copy-done.3, bf16[512,128]{1,0:T(8,128)(2,1)S(1)} %copy-done.2, bf16[1,3,512,512]{3,2,1,0:T(8,128)(2,1)S(1)} %copy-done, bf16[5,512,128]{2,1,0:T(8,128)(2,1)S(1)} %copy-done.1), custom_call_target="tpu_custom_call" | custom-call | flops 369098752 | bytes 1572864 | tf_op jit(solution)/shard_map/pallas_call | solution.py:224
  22.0 0.7 %copy.6 = f32[512,128]{1,0:T(8,128)} copy(f32[512,128]{1,0:T(8,128)S(1)} %shard_map.46) | data formatting | bytes 524288
Async XLA Ops:
  0.0 1.4 %copy-start = (bf16[1,3,512,512]{3,2,1,0:T(8,128)(2,1)S(1)}, bf16[1,3,512,512]{3,2,1,0:T(8,128)(2,1)}, u32[]{:S(2)}) copy-start(bf16[1,3,512,512]{3,2,1,0:T(8,128)(2,1)} %near_hbm.1) | copy-start | bytes 4718596
  1.4 1.1 %copy-start.1 = (bf16[5,512,128]{2,1,0:T(8,128)(2,1)S(1)}, bf16[5,512,128]{2,1,0:T(8,128)(2,1)}, u32[]{:S(2)}) copy-start(bf16[5,512,128]{2,1,0:T(8,128)(2,1)} %far_hbm.1) | copy-start | bytes 1966084
  2.5 0.9 %copy-start.2 = (bf16[512,128]{1,0:T(8,128)(2,1)S(1)}, bf16[512,128]{1,0:T(8,128)(2,1)}, u32[]{:S(2)}) copy-start(bf16[512,128]{1,0:T(8,128)(2,1)} %probes_hbm.1) | copy-start | bytes 393220
  3.4 0.7 %copy-start.3 = (s32[1,3]{1,0:T(1,128)S(1)}, s32[1,3]{1,0:T(1,128)}, u32[]{:S(2)}) copy-start(s32[1,3]{1,0:T(1,128)} %offsets.1) | copy-start | bytes 40

commit v2 on v1

--- a/solution.py
+++ b/solution.py
@@ -30,8 +30,8 @@
 
 
 def kernel(
-    levels, slabs, leaves, offsets, probes_hbm, near_hbm, far_hbm, out_hbm,
-    window, near, far, partial, arrived, piece, coupling, out,
+    levels, slabs, leaves, offsets_hbm, probes_hbm, near_hbm, far_hbm, out_hbm,
+    offsets, window, near, far, partial, arrived, piece, coupling, out,
     load_sem, out_sem, sum_send, sum_recv, piece_send, piece_recv, probe_send, probe_recv,
 ):
     slab, leaf = lax.axis_index("slab"), lax.axis_index("leaf")
@@ -52,8 +52,10 @@
     load_probes = pltpu.make_async_copy(probes_hbm, window.at[1], load_sem.at[0])
     load_far = pltpu.make_async_copy(far_hbm.at[pl.ds(0, levels)], far, load_sem.at[1])
     load_near = pltpu.make_async_copy(near_hbm.at[0], near, load_sem.at[2])
+    load_offsets = pltpu.make_async_copy(offsets_hbm, offsets, load_sem.at[3])
     load_probes.start()
     load_far.start()
+    load_offsets.start()
     load_near.start()
 
     has_low, has_high = me > 0, me < total - 1
@@ -169,6 +171,7 @@
     pl.when(has_high)(lambda: await_bytes(window.at[2], probe_recv.at[1]))
     pl.when(has_low)(lambda: await_bytes(window.at[0], probe_recv.at[0]))
     load_near.wait()
+    load_offsets.wait()
     members = near.shape[0]
     value = jnp.dot(near[0], window[offsets[0, 0] + 1], preferred_element_type=jnp.float32)
     for member in range(1, members):
@@ -224,9 +227,10 @@
     return pl.pallas_call(
         functools.partial(kernel, levels, slabs, leaves),
         out_shape=jax.ShapeDtypeStruct((points, columns), jnp.float32),
-        in_specs=[pl.BlockSpec(memory_space=pltpu.SMEM)] + [pl.BlockSpec(memory_space=pl.ANY)] * 3,
+        in_specs=[pl.BlockSpec(memory_space=pl.ANY)] * 4,
         out_specs=pl.BlockSpec(memory_space=pl.ANY),
         scratch_shapes=[
+            pltpu.SMEM((1, members), jnp.int32),
             pltpu.VMEM((3, points, columns), jnp.bfloat16),
             pltpu.VMEM((members, points, points), jnp.bfloat16),
             pltpu.VMEM((levels, points, rank), jnp.bfloat16),
@@ -235,7 +239,7 @@
             pltpu.VMEM((levels, columns, rank), jnp.bfloat16),
             pltpu.VMEM((levels, columns, rank), jnp.bfloat16),
             pltpu.VMEM((points, columns), jnp.float32),
-            pltpu.SemaphoreType.DMA((3,)),
+            pltpu.SemaphoreType.DMA((4,)),
             pltpu.SemaphoreType.DMA,
             pltpu.SemaphoreType.DMA((levels,)),
             pltpu.SemaphoreType.DMA((levels,)),
@@ -245,7 +249,7 @@
             pltpu.SemaphoreType.DMA((2,)),
         ],
         compiler_params=pltpu.CompilerParams(
-            collective_id=0, has_side_effects=True, vmem_limit_bytes=24 * 2**20
+            collective_id=0, has_side_effects=True, vmem_limit_bytes=60 * 2**20
         ),
         cost_estimate=pl.CostEstimate(flops=flops, bytes_accessed=2 * near_blocks.size, transcendentals=0),
     )(near_offsets, probes, near_blocks, far_basis)

time: 22.9 us -> 19.5 us (0.85)
  local copies, waits for them, and re-layouts: 4.76 us -> 1.67 us
  Pallas kernels: 18 us -> 17.7 us
    unnamed x9 -> x1, local copies, waits for them, and re-layouts: 4.76 us -> 1.67 us
    pallas_call x1, Pallas kernels: 18 us -> 17.7 us  [direct(): pl.pallas_call(functools.partial(kernel, levels, slabs, leaves), out_shap...]
where the time goes in v2:
time: 19.5 us; the launch traced here: 19.3 us
  Pallas kernels  17.7 us (91%)
  local copies, waits for them, and re-layouts  1.67 us (9%)
    pallas_call x1, Pallas kernels, direct(): pl.pallas_call(functools.partial(kernel, levels, slabs, leaves), out_shap...  17.7 us
    unnamed x1, local copies, waits for them, and re-layouts  1.67 us

profile of v2, /device:TPU:0, one launch (start us, length us, event | category | flops | bytes accessed | tf_op | source)
XLA Modules:
  0.0 19.3 jit_solution(17483617497884442009)
XLA Ops:
  0.0 17.7 %shard_map.46 = f32[512,128]{1,0:T(8,128)} custom-call(s32[1,3]{1,0:T(1,128)} %offsets_hbm.1, bf16[512,128]{1,0:T(8,128)(2,1)} %probes_hbm.1, bf16[1,3,512,512]{3,2,1,0:T(8,128)(2,1)} %near_hbm.1, bf16[5,512,128]{2,1,0:T(8,128)(2,1)} %far_hbm.1), custom_call_target="tpu_custom_call" | custom-call | flops 369098752 | bytes 1572864 | tf_op jit(solution)/shard_map/pallas_call | solution.py:227
  17.7 1.7 %copy.6 = f32[512,128]{1,0:T(8,128)} copy(f32[512,128]{1,0:T(8,128)} %shard_map.46) | data formatting | bytes 524288

commit v3 on v2

--- a/solution.py
+++ b/solution.py
@@ -30,8 +30,8 @@
 
 
 def kernel(
-    levels, slabs, leaves, offsets_hbm, probes_hbm, near_hbm, far_hbm, out_hbm,
-    offsets, window, near, far, partial, arrived, piece, coupling, out,
+    levels, slabs, leaves, offsets_hbm, probes_hbm, near_hbm, far_hbm, out_hbm, coupling,
+    offsets, window, near, far, partial, arrived, piece, out,
     load_sem, out_sem, sum_send, sum_recv, piece_send, piece_recv, probe_send, probe_recv,
 ):
     slab, leaf = lax.axis_index("slab"), lax.axis_index("leaf")
@@ -180,17 +180,10 @@
         )
     out[...] = value
 
+    store = pltpu.make_async_copy(out, out_hbm, out_sem)
+    store.start()
     for level in range(levels):
         await_bytes(coupling.at[level], piece_recv.at[level])
-    value = out[...]
-    for level in range(levels):
-        value = value + lax.dot_general(
-            far[level], coupling[level], (((1,), (1,)), ((), ())),
-            preferred_element_type=jnp.float32,
-        )
-    out[...] = value
-    store = pltpu.make_async_copy(out, out_hbm, out_sem)
-    store.start()
 
     await_bytes(piece.at[0], piece_send.at[0])
     for level in range(1, levels):
@@ -226,9 +219,12 @@
     flops = 2 * points * columns * (members * points + 2 * levels * rank)
     return pl.pallas_call(
         functools.partial(kernel, levels, slabs, leaves),
-        out_shape=jax.ShapeDtypeStruct((points, columns), jnp.float32),
+        out_shape=[
+            jax.ShapeDtypeStruct((points, columns), jnp.float32),
+            jax.ShapeDtypeStruct((levels, columns, rank), jnp.bfloat16),
+        ],
         in_specs=[pl.BlockSpec(memory_space=pl.ANY)] * 4,
-        out_specs=pl.BlockSpec(memory_space=pl.ANY),
+        out_specs=[pl.BlockSpec(memory_space=pl.ANY)] * 2,
         scratch_shapes=[
             pltpu.SMEM((1, members), jnp.int32),
             pltpu.VMEM((3, points, columns), jnp.bfloat16),
@@ -236,7 +232,6 @@
             pltpu.VMEM((levels, points, rank), jnp.bfloat16),
             pltpu.VMEM((levels, columns, rank), jnp.float32),
             arrived,
-            pltpu.VMEM((levels, columns, rank), jnp.bfloat16),
             pltpu.VMEM((levels, columns, rank), jnp.bfloat16),
             pltpu.VMEM((points, columns), jnp.float32),
             pltpu.SemaphoreType.DMA((4,)),
@@ -288,7 +283,10 @@
 def body(probes, near_blocks, near_offsets, far_basis):
     levels = far_basis.shape[0]
     first = min(levels, DIRECT_LEVELS)
-    output = direct(probes, near_blocks, near_offsets, far_basis, first)
+    near_sum, coupling = direct(probes, near_blocks, near_offsets, far_basis, first)
+    output = near_sum + jnp.einsum(
+        "lpr,lqr->pq", far_basis[:first], coupling, preferred_element_type=jnp.float32
+    )
     if levels > first:
         output = upper(output, probes, far_basis, first)
     return output

time: 19.5 us -> 18.8 us (0.964)
  matrix products: 0 us -> 2.08 us
  local copies, waits for them, and re-layouts: 1.67 us -> 0.01 us
  Pallas kernels: 17.7 us -> 16.5 us
    dot_general x0 -> x1, matrix products: none -> 2.08 us  [body(): jnp.einsum('lpr,lqr->pq', far_basis[:first], coupling, preferred_element_...]
    unnamed x1 -> x2, local copies, waits for them, and re-layouts: 1.67 us -> 0.01 us
    pallas_call x1, Pallas kernels: 17.7 us -> 16.5 us  [direct(): pl.pallas_call(functools.partial(kernel, levels, slabs, leaves), out_shap...]
where the time goes in v3:
time: 18.8 us; the launch traced here: 18.6 us
  Pallas kernels  16.5 us (88%)
  matrix products  2.08 us (11%)
    pallas_call x1, Pallas kernels, direct(): pl.pallas_call(functools.partial(kernel, levels, slabs, leaves), out_shap...  16.5 us
    dot_general x1, matrix products, body(): jnp.einsum('lpr,lqr->pq', far_basis[:first], coupling, preferred_element_...  2.08 us

profile of v3, /device:TPU:0, one launch (start us, length us, event | category | flops | bytes accessed | tf_op | source)
XLA Modules:
  0.0 18.6 jit_solution(12281834018021906153)
XLA Ops:
  0.0 0.0 copy-start
  0.0 16.5 %shard_map.46 = (f32[512,128]{1,0:T(8,128)}, bf16[5,128,128]{2,1,0:T(8,128)(2,1)}) custom-call(s32[1,3]{1,0:T(1,128)} %offsets_hbm.1, bf16[512,128]{1,0:T(8,128)(2,1)} %probes_hbm.1, bf16[1,3,512,512]{3,2,1,0:T(8,128)(2,1)} %near_hbm.1, bf16[5,512,128]{2,1,0:T(8,128)(2,1)} %far_hbm.1), custom_call_target="tpu_custom_call" | custom-call | flops 369098752 | bytes 1572864 | tf_op jit(solution)/shard_map/pallas_call | solution.py:220
  16.5 0.0 copy-done
  16.5 2.1 %fusion = f32[512,128]{1,0:T(8,128)} fusion(f32[512,128]{1,0:T(8,128)} %get-tuple-element.7, bf16[5,128,128]{2,1,0:T(8,128)(2,1)} %get-tuple-element.8, bf16[5,512,128]{2,1,0:T(8,128)(2,1)S(1)} %copy-done), kind=kOutput, calls=%fused_computation.1 | convolution fusion | flops 83951616 | bytes 1343488 | tf_op jit(solution)/shard_map/lpr,lqr->pq/dot_general | solution.py:287
Async XLA Ops:
  0.0 16.5 %copy-start = (bf16[5,512,128]{2,1,0:T(8,128)(2,1)S(1)}, bf16[5,512,128]{2,1,0:T(8,128)(2,1)}, u32[]{:S(2)}) copy-start(bf16[5,512,128]{2,1,0:T(8,128)(2,1)} %far_hbm.1) | copy-start | bytes 1966084

commit v4 on v3

v4 whole, which is shorter than its diff:
```python
import functools

import jax
import jax.numpy as jnp
from jax import lax
from jax.experimental import pallas as pl
from jax.experimental.pallas import tpu as pltpu
from jax.sharding import PartitionSpec as P

MESH = pl.DeviceIdType.MESH
DIRECT_LEVELS = 5


def flipped(index, mask):
    bit = 1
    result = index
    while bit <= mask:
        if mask & bit:
            result = result + bit * (1 - 2 * ((index // bit) % 2))
        bit *= 2
    return result


def kernel(
    levels, slabs, leaves, offsets_hbm, probes_hbm, near_hbm, far_hbm, out_hbm, coupling,
    offsets, window, near, far, partial, paired, arrived, piece, out,
    load_sem, out_sem, pair_send, pair_recv, relay_send, relay_recv,
    sum_send, sum_recv, piece_send, piece_recv, probe_send, probe_recv,
):
    slab, leaf = lax.axis_index("slab"), lax.axis_index("leaf")
    me = slab * leaves + leaf
    core = leaf % 2
    total = slabs * leaves
    group = 2**levels
    columns = partial.shape[1]

    def device(mask):
        return flipped(slab, mask // leaves), flipped(leaf, mask % leaves)

    def along(step):
        other = me + step
        return other // leaves, other % leaves

    load_probes = pltpu.make_async_copy(probes_hbm, window.at[1], load_sem.at[0])
    load_far = pltpu.make_async_copy(far_hbm.at[pl.ds(0, levels)], far, load_sem.at[1])
    load_near = pltpu.make_async_copy(near_hbm.at[0], near, load_sem.at[2])
    load_offsets = pltpu.make_async_copy(offsets_hbm, offsets, load_sem.at[3])
    load_probes.start()
    load_far.start()
    load_offsets.start()
    load_near.start()

    has_low, has_high = me > 0, me < total - 1
    barrier = pltpu.get_barrier_semaphore()
    for mask in [1] + list(range(2, group, 2)):
        pl.semaphore_signal(barrier, inc=1, device_id=device(mask), device_id_type=MESH)
    beside = jnp.where(core == 0, me > 0, me < total - 1)

    @pl.when(beside)
    def _():
        pl.semaphore_signal(barrier, inc=1, device_id=along(2 * core - 1), device_id_type=MESH)

    load_probes.wait()
    load_far.wait()
    turned = window[1].T
    for level in reversed(range(levels)):
        partial[level] = jnp.dot(turned, far[level], preferred_element_type=jnp.float32)
    piece[0] = partial[0].astype(jnp.bfloat16)

    pl.semaphore_wait(barrier, group // 2 + beside.astype(jnp.int32))

    def remote(source, target, send, recv, where):
        return pltpu.make_async_remote_copy(
            src_ref=source, dst_ref=target, send_sem=send, recv_sem=recv,
            device_id=where, device_id_type=MESH,
        )

    def height_of(level):
        return columns // 2 ** (level - 1)

    def rows_of(level, index):
        height = height_of(level)
        return pl.ds(pl.multiple_of((index % 2**level) // 2 * height, height), height)

    def await_bytes(ref, sem):
        pltpu.make_async_copy(ref, ref, sem).wait()

    def on_core(action):
        for side in range(2):
            owned = [level for level in reversed(range(1, levels)) if level % 2 == side]
            others = [level for level in reversed(range(1, levels)) if level % 2 != side]
            pl.when(core == side)(functools.partial(action, owned, others))

    def hand_over(owned, others):
        for level in others:
            remote(
                partial.at[level], paired.at[level],
                pair_send.at[level], pair_recv.at[level], device(1),
            ).start()

    on_core(hand_over)
    remote(piece.at[0], coupling.at[0], piece_send.at[0], piece_recv.at[0], device(1)).start()
    to_low = remote(window.at[1], window.at[2], probe_send.at[0], probe_recv.at[1], along(-1))
    to_high = remote(window.at[1], window.at[0], probe_send.at[1], probe_recv.at[0], along(1))
    pl.when(has_low)(to_low.start)
    pl.when(has_high)(to_high.start)

    def announce(level, value):
        rows = pl.ds(0, height_of(level))
        piece[level, rows] = (value * 2.0 ** (-0.5 * level)).astype(jnp.bfloat16)
        for mask in reversed(range(2**level, 2 ** (level + 1), 2)):
            remote(
                piece.at[level, rows], coupling.at[level, rows_of(level, me)],
                piece_send.at[level], piece_recv.at[level], device(mask),
            ).start()

    def reduce(owned, others):
        for level in owned:
            await_bytes(paired.at[level], pair_recv.at[level])
            value = partial[level] + paired[level]
            if level == 1:
                announce(level, value)
                continue
            partial[level] = value
            for mask in reversed(range(2, 2**level, 2)):
                remote(
                    partial.at[level, rows_of(level, flipped(me, mask))],
                    arrived[level - 2].at[mask // 2],
                    sum_send.at[level], sum_recv.at[level], device(mask),
                ).start()
        for level in owned:
            if level == 1:
                continue
            chips = 2 ** (level - 1)
            await_bytes(arrived[level - 2].at[pl.ds(1, chips - 1)], sum_recv.at[level])
            value = partial[level, rows_of(level, me)]
            for chip in range(1, chips):
                value = value + arrived[level - 2][chip]
            announce(level, value)

    on_core(reduce)

    @pl.when(jnp.logical_not(has_low))
    def _():
        window[0] = jnp.zeros_like(window[0])

    @pl.when(jnp.logical_not(has_high))
    def _():
        window[2] = jnp.zeros_like(window[2])

    pl.when(has_high)(lambda: await_bytes(window.at[2], probe_recv.at[1]))
    pl.when(has_low)(lambda: await_bytes(window.at[0], probe_recv.at[0]))
    load_near.wait()
    load_offsets.wait()
    members = near.shape[0]
    value = jnp.dot(near[0], window[offsets[0, 0] + 1], preferred_element_type=jnp.float32)
    for member in range(1, members):
        value = value + jnp.dot(
            near[member], window[offsets[0, member] + 1], preferred_element_type=jnp.float32
        )
    out[...] = value

    store = pltpu.make_async_copy(out, out_hbm, out_sem)
    store.start()

    def relay(owned, others):
        for level in reversed(owned):
            await_bytes(coupling.at[level], piece_recv.at[level])
            remote(
                coupling.at[level], coupling.at[level],
                relay_send.at[level], relay_recv.at[level], device(1),
            ).start()
        await_bytes(coupling.at[0], piece_recv.at[0])
        for level in others:
            await_bytes(partial.at[level], pair_send.at[level])
            await_bytes(coupling.at[level], relay_recv.at[level])
        for level in owned:
            if level > 1:
                await_bytes(partial.at[level, pl.ds(0, columns - height_of(level))], sum_send.at[level])
            await_bytes(coupling.at[level], piece_send.at[level])
            await_bytes(coupling.at[level], relay_send.at[level])

    on_core(relay)
    await_bytes(piece.at[0], piece_send.at[0])
    pl.when(has_low)(to_low.wait_send)
    pl.when(has_high)(to_high.wait_send)
    store.wait()


def direct(probes, near_blocks, near_offsets, far_basis, levels):
    points, columns = probes.shape
    rank = far_basis.shape[2]
    members = near_blocks.shape[1]
    slabs, leaves = lax.axis_size("slab"), lax.axis_size("leaf")
    arrived = [
        pltpu.VMEM((2 ** (level - 1), columns // 2 ** (level - 1), rank), jnp.float32)
        for level in range(2, levels)
    ]
    flops = 2 * points * columns * (members * points + 2 * levels * rank)
    return pl.pallas_call(
        functools.partial(kernel, levels, slabs, leaves),
        out_shape=[
            jax.ShapeDtypeStruct((points, columns), jnp.float32),
            jax.ShapeDtypeStruct((levels, columns, rank), jnp.bfloat16),
        ],
        in_specs=[pl.BlockSpec(memory_space=pl.ANY)] * 4,
        out_specs=[pl.BlockSpec(memory_space=pl.ANY)] * 2,
        scratch_shapes=[
            pltpu.SMEM((1, members), jnp.int32),
            pltpu.VMEM((3, points, columns), jnp.bfloat16),
            pltpu.VMEM((members, points, points), jnp.bfloat16),
            pltpu.VMEM((levels, points, rank), jnp.bfloat16),
            pltpu.VMEM((levels, columns, rank), jnp.float32),
            pltpu.VMEM((levels, columns, rank), jnp.float32),
            arrived,
            pltpu.VMEM((levels, columns, rank), jnp.bfloat16),
            pltpu.VMEM((points, columns), jnp.float32),
            pltpu.SemaphoreType.DMA((4,)),
            pltpu.SemaphoreType.DMA,
            pltpu.SemaphoreType.DMA((levels,)),
            pltpu.SemaphoreType.DMA((levels,)),
            pltpu.SemaphoreType.DMA((levels,)),
            pltpu.SemaphoreType.DMA((levels,)),
            pltpu.SemaphoreType.DMA((levels,)),
            pltpu.SemaphoreType.DMA((levels,)),
            pltpu.SemaphoreType.DMA((levels,)),
            pltpu.SemaphoreType.DMA((levels,)),
            pltpu.SemaphoreType.DMA((2,)),
            pltpu.SemaphoreType.DMA((2,)),
        ],
        compiler_params=pltpu.CompilerParams(
            collective_id=0, has_side_effects=True, vmem_limit_bytes=60 * 2**20
        ),
        cost_estimate=pl.CostEstimate(flops=flops, bytes_accessed=2 * near_blocks.size, transcendentals=0),
    )(near_offsets, probes, near_blocks, far_basis)


def swapped(value, axis, bit):
    mask = 2**bit
    pairs = [(source, source ^ mask) for source in range(lax.axis_size(axis))]
    return lax.ppermute(value, axis, pairs)


def upper(output, probes, far_basis, first):
    levels = far_basis.shape[0]
    partial_sums = {
        level: lax.dot_general(
            far_basis[level], probes, (((0,), (0,)), ((), ())), preferred_element_type=jnp.float32
        )
        for level in range(first, levels)
    }
    leaf_bits = lax.axis_size("leaf").bit_length() - 1
    for bit in range(levels):
        axis, axis_bit = ("leaf", bit) if bit < leaf_bits else ("slab", bit - leaf_bits)
        kept = [level for level in range(first, levels) if level >= bit]
        incoming = swapped(jnp.stack([partial_sums[level] for level in kept]), axis, axis_bit)
        for place, level in enumerate(kept):
            if level == bit:
                coupling = (incoming[place] * 2.0 ** (-0.5 * level)).astype(jnp.bfloat16)
                output = output + jnp.dot(
                    far_basis[level], coupling, preferred_element_type=jnp.float32
                )
            else:
                partial_sums[level] = partial_sums[level] + incoming[place]
    return output


def body(probes, near_blocks, near_offsets, far_basis):
    levels = far_basis.shape[0]
    first = min(levels, DIRECT_LEVELS)
    near_sum, coupling = direct(probes, near_blocks, near_offsets, far_basis, first)
    output = near_sum
    for level in range(first):
        output = output + lax.dot_general(
            far_basis[level], coupling[level], (((1,), (1,)), ((), ())),
            preferred_element_type=jnp.float32,
        )
    if levels > first:
        output = upper(output, probes, far_basis, first)
    return output


def solution(mesh):
    return jax.shard_map(
        body,
        mesh=mesh,
        in_specs=(
            P(("slab", "leaf"), None),
            P(("slab", "leaf"), None, None, None),
            P(("slab", "leaf"), None),
            P(None, ("slab", "leaf"), None),
        ),
        out_specs=P(("slab", "leaf"), None),
        check_vma=False,
    )
```

time: 18.8 us -> 23.4 us (1.24); the launches traced: 18.6 us -> 22.9 us
  matrix products: 2.08 us -> 5.64 us
  Pallas kernels: 16.5 us -> 17.2 us
    dot_general x1 -> x5, matrix products: 2.08 us -> 5.64 us  [body(): lax.dot_general(far_basis[level], coupling[level], (((1,), (1,)), ((), ()...]
    pallas_call x1, Pallas kernels: 16.5 us -> 17.2 us  [direct(): pl.pallas_call(functools.partial(kernel, levels, slabs, leaves), out_shap...]
where the time goes in v4:
time: 23.4 us; the launch traced here: 22.9 us
  Pallas kernels  17.2 us (74%)
  matrix products  5.64 us (24%)
    pallas_call x1, Pallas kernels, direct(): pl.pallas_call(functools.partial(kernel, levels, slabs, leaves), out_shap...  17.2 us
    dot_general x5, matrix products, body(): lax.dot_general(far_basis[level], coupling[level], (((1,), (1,)), ((), ()...  5.64 us

profile of v4, /device:TPU:0, one launch (start us, length us, event | category | flops | bytes accessed | tf_op | source)
XLA Modules:
  0.0 22.9 jit_solution(1687204928821217158)
XLA Ops:
  0.0 0.0 copy-start
  0.0 17.2 %shard_map.46 = (f32[512,128]{1,0:T(8,128)}, bf16[5,128,128]{2,1,0:T(8,128)(2,1)}) custom-call(s32[1,3]{1,0:T(1,128)} %offsets_hbm.1, bf16[512,128]{1,0:T(8,128)(2,1)} %probes_hbm.1, bf16[1,3,512,512]{3,2,1,0:T(8,128)(2,1)} %near_hbm.1, bf16[5,512,128]{2,1,0:T(8,128)(2,1)} %far_hbm.1), custom_call_target="tpu_custom_call" | custom-call | flops 369098752 | bytes 1572864 | tf_op jit(solution)/shard_map/pallas_call | solution.py:200
  17.2 0.0 copy-done
  17.3 1.2 %fusion.4 = f32[512,128]{1,0:T(8,128)S(1)} fusion(f32[512,128]{1,0:T(8,128)} %get-tuple-element.7, bf16[5,512,128]{2,1,0:T(8,128)(2,1)S(1)} %copy-done, bf16[5,128,128]{2,1,0:T(8,128)(2,1)} %get-tuple-element.8), kind=kOutput, calls=%fused_computation.9 | convolution fusion | flops 16842752 | bytes 688128 | tf_op jit(solution)/shard_map/dot_general | solution.py:274
  18.4 0.9 %fusion.3 = f32[512,128]{1,0:T(8,128)S(1)} fusion(f32[512,128]{1,0:T(8,128)S(1)} %fusion.4, bf16[5,512,128]{2,1,0:T(8,128)(2,1)S(1)} %copy-done, bf16[5,128,128]{2,1,0:T(8,128)(2,1)} %get-tuple-element.8), kind=kOutput, calls=%fused_computation.7 | convolution fusion | flops 16842752 | bytes 688128 | tf_op jit(solution)/shard_map/dot_general | solution.py:274
  19.4 0.9 %fusion.2 = f32[512,128]{1,0:T(8,128)S(1)} fusion(f32[512,128]{1,0:T(8,128)S(1)} %fusion.3, bf16[5,512,128]{2,1,0:T(8,128)(2,1)S(1)} %copy-done, bf16[5,128,128]{2,1,0:T(8,128)(2,1)} %get-tuple-element.8), kind=kOutput, calls=%fused_computation.5 | convolution fusion | flops 16842752 | bytes 688128 | tf_op jit(solution)/shard_map/dot_general | solution.py:274
  20.3 0.9 %fusion.1 = f32[512,128]{1,0:T(8,128)S(1)} fusion(f32[512,128]{1,0:T(8,128)S(1)} %fusion.2, bf16[5,512,128]{2,1,0:T(8,128)(2,1)S(1)} %copy-done, bf16[5,128,128]{2,1,0:T(8,128)(2,1)} %get-tuple-element.8), kind=kOutput, calls=%fused_computation.3 | convolution fusion | flops 16842752 | bytes 688128 | tf_op jit(solution)/shard_map/dot_general | solution.py:274
  21.3 1.7 %fusion = f32[512,128]{1,0:T(8,128)} fusion(f32[512,128]{1,0:T(8,128)S(1)} %fusion.1, bf16[5,512,128]{2,1,0:T(8,128)(2,1)S(1)} %copy-done, bf16[5,128,128]{2,1,0:T(8,128)(2,1)} %get-tuple-element.8), kind=kOutput, calls=%fused_computation.1 | convolution fusion | flops 16842752 | bytes 688128 | tf_op jit(solution)/shard_map/dot_general | solution.py:274
Async XLA Ops:
  0.0 17.3 %copy-start = (bf16[5,512,128]{2,1,0:T(8,128)(2,1)S(1)}, bf16[5,512,128]{2,1,0:T(8,128)(2,1)}, u32[]{:S(2)}) copy-start(bf16[5,512,128]{2,1,0:T(8,128)(2,1)} %far_hbm.1) | copy-start | bytes 1966084

commit v5 on v3

--- a/solution.py
+++ b/solution.py
@@ -97,6 +97,11 @@
             chunk = chunk // 2
         height = rank // count
         return pl.ds(pl.multiple_of(chunk * height, height), height)
+
+    to_low = remote(window.at[1], window.at[2], probe_send.at[0], probe_recv.at[1], along(-1))
+    to_high = remote(window.at[1], window.at[0], probe_send.at[1], probe_recv.at[0], along(1))
+    pl.when(has_low)(to_low.start)
+    pl.when(has_high)(to_high.start)
 
     for level in reversed(range(1, levels)):
         parity = owner_parity(level)
@@ -128,11 +133,6 @@
                     send()
 
     remote(piece.at[0], coupling.at[0], piece_send.at[0], piece_recv.at[0], device(1)).start()
-
-    to_low = remote(window.at[1], window.at[2], probe_send.at[0], probe_recv.at[1], along(-1))
-    to_high = remote(window.at[1], window.at[0], probe_send.at[1], probe_recv.at[0], along(1))
-    pl.when(has_low)(to_low.start)
-    pl.when(has_high)(to_high.start)
 
     def await_bytes(ref, sem):
         pltpu.make_async_copy(ref, ref, sem).wait()

time: 18.8 us -> 19.9 us (1.059)
  Pallas kernels: 16.5 us -> 17.6 us
    pallas_call x1, Pallas kernels: 16.5 us -> 17.6 us  [direct(): pl.pallas_call(functools.partial(kernel, levels, slabs, leaves), out_shap...]
where the time goes in v5:
time: 19.9 us; the launch traced here: 19.7 us
  Pallas kernels  17.6 us (88%)
  matrix products  2.08 us (10%)
    pallas_call x1, Pallas kernels, direct(): pl.pallas_call(functools.partial(kernel, levels, slabs, leaves), out_shap...  17.6 us
    dot_general x1, matrix products, body(): jnp.einsum('lpr,lqr->pq', far_basis[:first], coupling, preferred_element_...  2.08 us

profile of v5, /device:TPU:0, one launch (start us, length us, event | category | flops | bytes accessed | tf_op | source)
XLA Modules:
  0.0 19.7 jit_solution(13249392555177544926)
XLA Ops:
  0.0 0.0 copy-start
  0.0 17.6 %shard_map.46 = (f32[512,128]{1,0:T(8,128)}, bf16[5,128,128]{2,1,0:T(8,128)(2,1)}) custom-call(s32[1,3]{1,0:T(1,128)} %offsets_hbm.1, bf16[512,128]{1,0:T(8,128)(2,1)} %probes_hbm.1, bf16[1,3,512,512]{3,2,1,0:T(8,128)(2,1)} %near_hbm.1, bf16[5,512,128]{2,1,0:T(8,128)(2,1)} %far_hbm.1), custom_call_target="tpu_custom_call" | custom-call | flops 369098752 | bytes 1572864 | tf_op jit(solution)/shard_map/pallas_call | solution.py:220
  17.6 0.0 copy-done
  17.6 2.1 %fusion = f32[512,128]{1,0:T(8,128)} fusion(f32[512,128]{1,0:T(8,128)} %get-tuple-element.7, bf16[5,128,128]{2,1,0:T(8,128)(2,1)} %get-tuple-element.8, bf16[5,512,128]{2,1,0:T(8,128)(2,1)S(1)} %copy-done), kind=kOutput, calls=%fused_computation.1 | convolution fusion | flops 83951616 | bytes 1343488 | tf_op jit(solution)/shard_map/lpr,lqr->pq/dot_general | solution.py:287
Async XLA Ops:
  0.0 17.6 %copy-start = (bf16[5,512,128]{2,1,0:T(8,128)(2,1)S(1)}, bf16[5,512,128]{2,1,0:T(8,128)(2,1)}, u32[]{:S(2)}) copy-start(bf16[5,512,128]{2,1,0:T(8,128)(2,1)} %far_hbm.1) | copy-start | bytes 1966084

commit v6 on v3

--- a/solution.py
+++ b/solution.py
@@ -153,7 +153,7 @@
                 piece_send.at[level], piece_recv.at[level], device(mask),
             ).start()
 
-    for level in reversed(range(1, levels)):
+    for level in range(1, levels):
         parity = owner_parity(level)
         if parity is None:
             finish(level)

time: 18.8 us -> 18.5 us (0.984)
  Pallas kernels: 16.5 us -> 16.3 us
    pallas_call x1, Pallas kernels: 16.5 us -> 16.3 us  [direct(): pl.pallas_call(functools.partial(kernel, levels, slabs, leaves), out_shap...]
where the time goes in v6:
time: 18.5 us; the launch traced here: 18.4 us
  Pallas kernels  16.3 us (88%)
  matrix products  2.07 us (11%)
    pallas_call x1, Pallas kernels, direct(): pl.pallas_call(functools.partial(kernel, levels, slabs, leaves), out_shap...  16.3 us
    dot_general x1, matrix products, body(): jnp.einsum('lpr,lqr->pq', far_basis[:first], coupling, preferred_element_...  2.07 us

profile of v6, /device:TPU:0, one launch (start us, length us, event | category | flops | bytes accessed | tf_op | source)
XLA Modules:
  0.0 18.4 jit_solution(4483808310620858856)
XLA Ops:
  0.0 0.0 copy-start
  0.0 16.3 %shard_map.46 = (f32[512,128]{1,0:T(8,128)}, bf16[5,128,128]{2,1,0:T(8,128)(2,1)}) custom-call(s32[1,3]{1,0:T(1,128)} %offsets_hbm.1, bf16[512,128]{1,0:T(8,128)(2,1)} %probes_hbm.1, bf16[1,3,512,512]{3,2,1,0:T(8,128)(2,1)} %near_hbm.1, bf16[5,512,128]{2,1,0:T(8,128)(2,1)} %far_hbm.1), custom_call_target="tpu_custom_call" | custom-call | flops 369098752 | bytes 1572864 | tf_op jit(solution)/shard_map/pallas_call | solution.py:220
  16.3 0.0 copy-done
  16.3 2.1 %fusion = f32[512,128]{1,0:T(8,128)} fusion(f32[512,128]{1,0:T(8,128)} %get-tuple-element.7, bf16[5,128,128]{2,1,0:T(8,128)(2,1)} %get-tuple-element.8, bf16[5,512,128]{2,1,0:T(8,128)(2,1)S(1)} %copy-done), kind=kOutput, calls=%fused_computation.1 | convolution fusion | flops 83951616 | bytes 1343488 | tf_op jit(solution)/shard_map/lpr,lqr->pq/dot_general | solution.py:287
Async XLA Ops:
  0.0 16.3 %copy-start = (bf16[5,512,128]{2,1,0:T(8,128)(2,1)S(1)}, bf16[5,512,128]{2,1,0:T(8,128)(2,1)}, u32[]{:S(2)}) copy-start(bf16[5,512,128]{2,1,0:T(8,128)(2,1)} %far_hbm.1) | copy-start | bytes 1966084
